TPU v7x, 256 devices: a whole 4x4x8 slice. The times are simulated.
256 devices in a mesh: item: 8 (over z), user: 16 (over x, y), tp: 2 (over core).
Axes of the slice: x: 4, y: 4, z: 8, core: 2. Of those that a mesh axis runs over, the one named last changes fastest.
Arguments:
- item_states: bfloat16 [2048, 4096], P('item', ('user', 'tp')), may hold values from -6 to 6
- w_gate: bfloat16 [4096, 8448], P(None, ('user', 'tp')), may hold values from -0.09375 to 0.09375
- w_up: bfloat16 [4096, 8448], P(None, ('user', 'tp')), may hold values from -0.09375 to 0.09375
- w_down: bfloat16 [8448, 4096], P(('user', 'tp')), may hold values from -0.0625 to 0.0625
- w_qkv: bfloat16 [4096, 3, 2048], P(None, None, ('item', 'tp')), may hold values from -0.09375 to 0.09375
- w_out: bfloat16 [2048, 4096], P(('item', 'tp')), may hold values from -0.125 to 0.125
- hist_ids: int32 [16, 256], P('user'), may hold values from 0 to 2047
- hist_lengths: int32 [16, 16], P('user'), may hold values from 1 to 64, 256 in all within a row
- neg_ids: int32 [16, 384], P('user'), may hold values from 0 to 2047
Outputs:
- loss: float32 [16], P('user')
- user_out: bfloat16 [16, 256, 4096], P('user')
- item_grad: float32 [2048, 4096], P(('item', 'user'), 'tp')
Inputs may be any that keep to these rules, and one draw needn't show every extreme that they name: Each row of hist_lengths sums to 256; the tokens of a shard's users stand one after another in hist_ids.
All inputs are finite; a program needn't handle non-finite values.
Results may differ from a plain program's by a relative error of at most 0.015.
Values may be sent and summed in bfloat16 or wider, within the bound.
No kernel may reach another device: no remote copies, remote signals or barrier semaphores. Data moves between devices by JAX's collectives and lax.ppermute only.
A program may use at most 128 MiB of HBM per device.

v0:
```python
import functools

import jax
import jax.numpy as jnp
from jax import lax
from jax.experimental import pallas as pl
from jax.experimental.pallas import tpu as pltpu
from jax.sharding import PartitionSpec as P

D = 4096
HD = 128
LANE = 128

masked_score = -1e30
f32 = jnp.float32
bf16 = jnp.bfloat16

VMEM = pl.BlockSpec(memory_space=pltpu.VMEM)
SMEM = pl.BlockSpec(memory_space=pltpu.SMEM)
ANY = pl.BlockSpec(memory_space=pl.ANY)
HBM = pl.BlockSpec(memory_space=pltpu.HBM)
DMAS = pltpu.SemaphoreType.DMA


def call(kernel, out_shape, in_specs, args, scratch=(), out_specs=None, vmem=12 << 20, flops=0, moved=0):
    if out_specs is None:
        out_specs = tuple(VMEM for _ in out_shape) if isinstance(out_shape, tuple) else VMEM
    return pl.pallas_call(
        kernel,
        out_shape=out_shape,
        in_specs=in_specs,
        out_specs=out_specs,
        scratch_shapes=list(scratch),
        compiler_params=pltpu.CompilerParams(vmem_limit_bytes=vmem),
        cost_estimate=pl.CostEstimate(flops=flops, bytes_accessed=moved, transcendentals=0),
    )(*args)


def run(copies):
    for copy in copies:
        copy.start()
    for copy in copies:
        copy.wait()


def dot(a, b):
    return jnp.dot(a, b, preferred_element_type=f32)


def dot_nt(a, b):
    return lax.dot_general(a, b, (((1,), (1,)), ((), ())), preferred_element_type=f32)


def dot_tn(a, b):
    return lax.dot_general(a, b, (((0,), (0,)), ((), ())), preferred_element_type=f32)


def aligned(start, unit):
    return pl.multiple_of(start, unit)


def gate_up(first, states_ref, gate_ref, up_ref, rows):
    chunks = states_ref.shape[0]
    states = jnp.concatenate([states_ref[u, :rows] for u in range(chunks)], axis=1)

    def side(ref):
        blocks = [ref[:, pl.ds(aligned((2 * u + first) * LANE, LANE), LANE)] for u in range(chunks)]
        return dot_nt(jnp.concatenate(blocks, axis=1), states)

    return side(gate_ref), side(up_ref)


def ffn_near_kernel(tp_ref, mine_ref, gate_ref, up_ref, gate_out, up_out):
    gate_out[...], up_out[...] = gate_up(tp_ref[0], mine_ref, gate_ref, up_ref, gate_out.shape[1])


def ffn_kernel(tp_ref, other_ref, gate_near, up_near, gate_ref, up_ref, down_ref, hidden_ref, send_ref):
    tp = tp_ref[0]
    half = D // 2
    gate, up = gate_up(1 - tp, other_ref, gate_ref, up_ref, hidden_ref.shape[0])
    gate = gate_near[...] + gate
    up = up_near[...] + up
    hidden = jnp.transpose(gate / (1.0 + jnp.exp(-gate)) * up).astype(bf16)
    hidden_ref[...] = hidden
    part = dot(hidden, down_ref[:, pl.ds(aligned((1 - tp) * half, half), half)]).astype(bf16)
    for u in range(send_ref.shape[0]):
        send_ref[u] = part[:, u * LANE : (u + 1) * LANE]


def down_kernel(tp_ref, hidden_ref, down_ref, got_ref, out_ref):
    half = D // 2
    part = dot(hidden_ref[...], down_ref[:, pl.ds(aligned(tp_ref[0] * half, half), half)])
    for u in range(out_ref.shape[0]):
        out_ref[u] = (part[:, u * LANE : (u + 1) * LANE] + got_ref[u].astype(f32)).astype(bf16)


def pick_kernel(ids_ref, emb_ref, out_ref):
    shards, rows = emb_ref.shape[0], emb_ref.shape[1]
    users, picks = out_ref.shape[0], out_ref.shape[1]
    group = shards // 2
    sides = [emb_ref[n * group : (n + 1) * group].reshape(group * rows, LANE) for n in range(2)]
    items = jnp.concatenate(sides, axis=1)
    slots = lax.broadcasted_iota(jnp.int32, (picks, rows), 1).astype(f32).astype(bf16)
    one, zero = jnp.ones((), bf16), jnp.zeros((), bf16)
    for u in range(users):
        ids = jnp.transpose(ids_ref[u])
        upper = ids[:, 0:1] >= group
        shard = jnp.broadcast_to(jnp.where(upper, ids[:, 0:1] - group, ids[:, 0:1]), (picks, rows)).astype(bf16)
        slot = jnp.broadcast_to(ids[:, 1:2], (picks, rows)).astype(bf16)
        here = jnp.where(slot == slots, one, zero)
        select = jnp.concatenate([jnp.where(shard == k, here, zero) for k in range(group)], axis=1)
        found = dot(select, items)
        out_ref[u] = jnp.where(upper, found[:, LANE:], found[:, :LANE]).astype(bf16)


def pick(ids, emb):
    users, picks = ids.shape[0], ids.shape[2]
    ids = jnp.concatenate([ids, jnp.zeros((users, 6, picks), f32)], axis=1)
    return call(
        pick_kernel,
        jax.ShapeDtypeStruct((users, picks, LANE), bf16),
        [VMEM, VMEM],
        (ids, emb),
        flops=2 * users * picks * emb.shape[1] * emb.shape[0] * LANE,
        moved=users * picks * LANE * 6,
    )


def project(half, tokens_ref, w_ref):
    rows = pl.ds(aligned(half * (D // 2), D // 2), D // 2)
    states = jnp.concatenate([tokens_ref[n] for n in range(tokens_ref.shape[0])], axis=1)
    return dot(states, jnp.concatenate([w_ref[j, rows, :] for j in range(3)], axis=1))


def project_kernel(half_ref, tokens_ref, w_ref, out_ref):
    out_ref[...] = project(half_ref[0], tokens_ref, w_ref)


def attend_kernel(half_ref, tokens_ref, w_ref, part_ref, allowed_ref, out_ref):
    projected = (part_ref[...] + project(half_ref[0], tokens_ref, w_ref)).astype(bf16)
    query, key, value = projected[:, :HD], projected[:, HD : 2 * HD], projected[:, 2 * HD :]
    scores = dot_nt(query, key) * HD ** (-0.5)
    scores = jnp.where(allowed_ref[...] > 0, scores, masked_score)
    weights = jnp.exp(scores - jnp.max(scores, axis=-1, keepdims=True))
    weights = (weights / jnp.sum(weights, axis=-1, keepdims=True)).astype(bf16)
    out_ref[...] = dot(weights, value).astype(bf16)


def fetch_kernel(shards, tp_ref, *refs):
    pieces, far, outs, sems = refs[: shards - 1], refs[shards - 1 : shards + 1], refs[shards + 1 : -1], refs[-1]
    width = outs[0].shape[1]
    rows = outs[0].shape[0] // shards
    copies = []
    for n, out_ref in enumerate(outs):
        half = tp_ref[0] if n else 1 - tp_ref[0]
        cols = pl.ds(aligned(half * width, width), width)
        for k, piece in enumerate(pieces):
            copies.append((piece.at[:, cols], out_ref.at[pl.ds(k * rows, rows)]))
        for k, piece in enumerate(far):
            first = (shards - 1) * rows + k * (rows // 2)
            copies.append((piece.at[:, cols], out_ref.at[pl.ds(first, rows // 2)]))
    run([pltpu.make_async_copy(src, dst, sems.at[n]) for n, (src, dst) in enumerate(copies)])


def mix_kernel(shards, *refs):
    heads, (w_ref, out_ref) = refs[:shards], refs[shards:]
    states = jnp.concatenate([ref[...] for ref in heads], axis=1)
    out_ref[...] = dot(states, w_ref[...]).astype(out_ref.dtype)


def user_kernel(own_ref, got_ref, token_ref, neg_ref, user_ref, out_ref):
    negs = neg_ref.shape[1]
    user_ref[...] = (own_ref[...] + got_ref[...].astype(f32)).astype(bf16)
    negatives = jnp.concatenate([neg_ref[u] for u in range(neg_ref.shape[0])], axis=1)
    out_ref[:, :negs] = dot_nt(user_ref[...], negatives)
    product = 0.0
    steps = token_ref.shape[1]
    for u in range(token_ref.shape[0]):
        following = pltpu.roll(token_ref[u].astype(f32), steps - 1, 0)
        product += user_ref[:, u * LANE : (u + 1) * LANE].astype(f32) * following
    out_ref[:, negs:] = product


def grad_kernel(
    pairs, shard_pairs, near_ref, far_ref, usable_ref, next_ref, slot_ref, user_ref, loss_ref, out_ref, buf, sems
):
    negs = slot_ref.shape[0]
    steps = near_ref.shape[0]
    rows = out_ref.shape[0]
    scale = D ** (-0.5)
    both = near_ref[...] + far_ref[...]
    negative = both[:, :negs] * scale
    positive = jnp.sum(both[:, negs:], axis=1, keepdims=True) * scale
    usable = usable_ref[...]
    row_max = jnp.maximum(positive, jnp.max(negative, axis=1, keepdims=True))
    exp_total = jnp.exp(positive - row_max) + jnp.sum(jnp.exp(negative - row_max), axis=1, keepdims=True)
    log_total = row_max + jnp.log(exp_total)
    loss = jnp.sum(jnp.where(usable > 0, log_total - positive, 0.0)) / shard_pairs
    loss_ref[...] = jnp.full(loss_ref.shape, loss, f32)
    usable_f = usable / pairs
    pos_grad = usable_f * (jnp.exp(positive - log_total) - 1.0)
    neg_grad = (usable_f * jnp.exp(negative - log_total)).astype(bf16)
    neg_pick = (slot_ref[...] == lax.broadcasted_iota(jnp.int32, (negs, rows), 1)).astype(f32).astype(bf16)
    pos_pick = next_ref[...] == lax.broadcasted_iota(jnp.int32, (steps, rows), 1)
    grad = (dot(neg_grad, neg_pick) + jnp.where(pos_pick, pos_grad, 0.0)).astype(bf16)
    grad = jnp.transpose(grad)
    copies = []
    block = rows // 2
    for n, first in enumerate(range(0, rows, block)):
        buf[first : first + block] = (dot(grad[first : first + block], user_ref[...]) * scale).astype(bf16)
        copies.append(
            pltpu.make_async_copy(buf.at[pl.ds(first, block)], out_ref.at[pl.ds(first, block)], sems.at[n])
        )
        copies[-1].start()
    for copy in copies:
        copy.wait()


def segment_of(lengths, seq_steps):
    user_ends = jnp.cumsum(lengths)
    position = jnp.arange(seq_steps, dtype=jnp.int32)
    return jnp.sum((position[:, None] >= user_ends[None, :]).astype(jnp.int32), axis=1)


def exchange(x):
    return lax.ppermute(x, "tp", [(0, 1), (1, 0)])


def spread(x, axis):
    copies = jnp.broadcast_to(x[None], (lax.axis_size(axis),) + x.shape)
    return lax.all_to_all(copies, axis, 0, 0, tiled=True)


def ring(shards, shift):
    return [(i, (i + shift) % shards) for i in range(shards)]


def body(item_states, w_gate, w_up, w_down, w_qkv, w_out, hist_ids, hist_lengths, neg_ids):
    row_count = item_states.shape[0]
    users, shards = lax.axis_size("user"), lax.axis_size("item")
    half = D // 2
    tp = lax.axis_index("tp").astype(jnp.int32).reshape(1)
    hist_row, neg_row = hist_ids[0], neg_ids[0]
    seq_steps, negs = hist_row.shape[0], neg_row.shape[0]

    right = functools.partial(lax.ppermute, axis_name="item", perm=ring(shards, 1))
    left = functools.partial(lax.ppermute, axis_name="item", perm=ring(shards, -1))
    pieces = [w_out, right(w_out), left(w_out)]

    named = jnp.concatenate([hist_row, neg_row])
    coded = jnp.stack([named // row_count, named % row_count]).reshape(-1, LANE)
    coded = jnp.pad(coded, ((0, -coded.shape[0] % 16), (0, 0))).astype(bf16)
    mine = spread(jnp.concatenate([item_states, coded], axis=0), "user")
    mine, *pieces[-2:] = lax.optimization_barrier((mine, *pieces[-2:]))
    pieces += [right(pieces[-2]), left(pieces[-1])]
    other = exchange(mine)
    all_ids = mine[:, row_count:].reshape(users, -1)[:, : 2 * (seq_steps + negs)].astype(f32)
    all_ids = all_ids.reshape(users, 2, seq_steps + negs)

    units = w_gate.shape[1]
    gate_near, up_near = call(
        ffn_near_kernel,
        (jax.ShapeDtypeStruct((units, row_count), f32),) * 2,
        [SMEM] + [VMEM] * 3,
        (tp, mine, w_gate.T, w_up.T),
        flops=2 * row_count * units * D,
        moved=4 * units * D,
    )
    hidden, send = call(
        ffn_kernel,
        (
            jax.ShapeDtypeStruct((row_count, units), bf16),
            jax.ShapeDtypeStruct((users, row_count, LANE), bf16),
        ),
        [SMEM] + [VMEM] * 6,
        (tp, other, gate_near, up_near, w_gate.T, w_up.T, w_down),
        flops=3 * row_count * units * D,
        moved=6 * units * D,
    )
    got = exchange(send)
    partial = call(
        down_kernel,
        jax.ShapeDtypeStruct((users, row_count, LANE), bf16),
        [SMEM] + [VMEM] * 3,
        (tp, hidden, w_down, got),
        flops=row_count * units * D,
        moved=units * D,
    )
    partials = lax.all_to_all(partial, "user", 0, 0, tiled=True)
    partials, *pieces[-2:] = lax.optimization_barrier((partials, *pieces[-2:]))
    pieces += [right(pieces[-2]), left(pieces[-1])]
    emb = jnp.sum(partials.astype(f32), axis=0).astype(bf16)

    all_emb = spread(emb, "item")
    picked = pick(all_ids[:, :, :seq_steps], all_emb)
    picked, neg_ids_all = lax.optimization_barrier((picked, all_ids[:, :, seq_steps:]))
    picked_negatives = pick(neg_ids_all, all_emb)
    tokens = lax.all_to_all(picked, "user", 0, 0, tiled=True)
    segment = segment_of(hist_lengths[0], seq_steps)
    position = jnp.arange(seq_steps, dtype=jnp.int32)
    allowed = (segment[:, None] == segment[None, :]) & (position[:, None] >= position[None, :])
    allowed = allowed.astype(f32)
    usable = jnp.concatenate([segment[:-1] == segment[1:], jnp.zeros((1,), jnp.bool_)]).astype(f32)[:, None]
    item_base = lax.axis_index("item").astype(jnp.int32) * row_count
    next_slot = (jnp.concatenate([hist_row[1:], hist_row[:1]]) - item_base)[:, None]
    neg_slot = (neg_row - item_base)[:, None]
    rows = w_out.shape[0] // 2
    ends = [pieces[-2][:rows], pieces[-1][rows:]]
    masks = (allowed, usable, next_slot, neg_slot)
    tokens, picked_negatives, ends, masks = lax.optimization_barrier((tokens, picked_negatives, ends, masks))
    allowed, usable, next_slot, neg_slot = masks
    far = [right(ends[0]), left(ends[1])]
    other_tokens = exchange(tokens)
    negatives = lax.all_to_all(picked_negatives, "user", 0, 0, tiled=True)

    qkv = w_qkv.transpose(1, 0, 2)
    qkv_width = qkv.shape[0] * qkv.shape[2]
    part = call(
        project_kernel,
        jax.ShapeDtypeStruct((seq_steps, qkv_width), f32),
        [SMEM] + [VMEM] * 2,
        (tp, tokens, qkv),
        flops=seq_steps * D * qkv_width,
        moved=D * qkv_width,
    )
    attended = call(
        attend_kernel,
        jax.ShapeDtypeStruct((seq_steps, HD), bf16),
        [SMEM] + [VMEM] * 4,
        (1 - tp, other_tokens, qkv, part, allowed),
        flops=seq_steps * D * qkv_width,
        moved=D * qkv_width,
    )
    shifts = [0, 1, -1, 2, -2, 3, -3, 4]
    heads = [attended] + [lax.ppermute(attended, "item", ring(shards, k)) for k in shifts[1:]]
    w_send, w_keep = call(
        functools.partial(fetch_kernel, shards),
        (jax.ShapeDtypeStruct((shards * w_out.shape[0], half), bf16),) * 2,
        [SMEM] + [ANY] * (shards + 1),
        [tp] + pieces + far,
        scratch=[DMAS((2 * shards + 2,))],
        moved=4 * shards * w_out.shape[0] * D,
    )

    def mixed(w, kind):
        return call(
            functools.partial(mix_kernel, shards),
            jax.ShapeDtypeStruct((seq_steps, half), kind),
            [VMEM] * (shards + 1),
            heads + [w],
            flops=seq_steps * half * D // 2,
            moved=half * D // 2,
        )

    got_user = exchange(mixed(w_send, bf16))
    own_user = mixed(w_keep, f32)
    user_half, near = call(
        user_kernel,
        (
            jax.ShapeDtypeStruct((seq_steps, half), bf16),
            jax.ShapeDtypeStruct((seq_steps, negs + LANE), f32),
        ),
        [VMEM] * 4,
        (own_user, got_user, tokens, negatives),
        flops=seq_steps * negs * D,
        moved=negs * D,
    )
    near_other = exchange(near)
    near_other, sent_half = lax.optimization_barrier((near_other, user_half))
    other_half = exchange(sent_half)
    shard_pairs = seq_steps - hist_lengths.shape[1]
    loss, item_part = call(
        functools.partial(grad_kernel, float(users * shard_pairs), float(shard_pairs)),
        (
            jax.ShapeDtypeStruct((8, LANE), f32),
            jax.ShapeDtypeStruct((row_count, half), bf16),
        ),
        [VMEM] * 6,
        (near, near_other, usable, next_slot, neg_slot, user_half),
        scratch=[pltpu.VMEM((row_count, half), bf16), DMAS((2,))],
        out_specs=(VMEM, HBM),
        flops=2 * seq_steps * row_count * half,
        moved=row_count * half * 2,
    )
    parts = lax.all_to_all(item_part.reshape(users, row_count // users, half), "user", 0, 0, tiled=True)
    low = jnp.where(tp[0] == 0, user_half, other_half)
    high = jnp.where(tp[0] == 0, other_half, user_half)
    user_out = jnp.concatenate([low, high], axis=1)[None]
    parts, user_out = lax.optimization_barrier((parts, user_out))
    item_grad = jnp.sum(parts.astype(f32), axis=0)
    return (loss[0, :1], user_out, item_grad)


def solution(mesh):
    placed = (
        P("item", ("user", "tp")),
        P(None, ("user", "tp")),
        P(None, ("user", "tp")),
        P(("user", "tp"), None),
        P(None, None, ("item", "tp")),
        P(("item", "tp"), None),
        P("user", None),
        P("user", None),
        P("user", None),
    )
    return jax.shard_map(
        body,
        mesh=mesh,
        in_specs=placed,
        out_specs=(P("user"), P("user", None, None), P(("item", "user"), "tp")),
        check_vma=False,
    )
```

profile of v0, /device:TPU:32, one launch (start us, length us, event | category | flops | bytes accessed | tf_op | source)
XLA Modules:
  0.0 186.4 jit_solution(10409673863079193122)
XLA Ops:
  0.6 2.0 %collective-permute-start = (bf16[128,4096]{1,0:T(8,128)(2,1)}, bf16[128,4096]{1,0:T(8,128)(2,1)}, u32[]{:S(2)}, u32[]{:S(2)}) collective-permute-start(bf16[128,4096]{1,0:T(8,128)(2,1)} %refs_0_.1), channel_id=1, source_target_pairs={{0,32},{32,64},{64,96},{96,128},{128,160},{160,192},{192,224},{224... | collective-permute-start | bytes 3145736 | tf_op jit(solution)/shard_map/ppermute | solution.py:248
  2.7 0.7 constant_dynamic-update-slice_fusion.1
  3.4 0.7 subtract_bitcast_fusion
  4.2 0.8 fusion.3
  5.2 24.3 %all_to_all.30.mine_ref = bf16[16,272,128]{2,1,0:T(8,128)(2,1)S(1)} all-to-all(bf16[16,272,128]{2,1,0:T(8,128)(2,1)S(1)} %broadcast_in_dim.6), channel_id=1, replica_groups=mesh['item'=8,'user'=16,'tp'=2] {'user'}, dimensions={0} | all-to-all | bytes 2228224 | tf_op jit(solution)/shard_map/all_to_all | solution.py:231
  29.5 1.6 copy-done.3
  31.1 0.8 shard_map.112
  31.9 0.4 collective-permute-done.2.other_ref
  32.4 0.4 copy-done.1
  32.7 2.8 %shard_map.113 = (bf16[256,264]{1,0:T(8,128)(2,1)S(1)}, bf16[16,256,128]{2,1,0:T(8,128)(2,1)S(1)}) custom-call(s32[1]{0:T(128)} %bitcast.tp_ref.half_ref, bf16[16,272,128]{2,1,0:T(8,128)(2,1)} %collective-permute-done.2.other_ref, f32[264,256]{1,0:T(8,128)S(1)} %get-tuple-element.34.gate_near, f32[264,256]{1,0:T(8,128)S(1)} %get-tuple-element.35.up_near, ...), custom_call_target="tpu_custom_call" | custom-call | flops 830472192 | bytes 6488064 | tf_op jit(solution)/shard_map/pallas_call | solution.py:28
  35.5 0.6 collective-permute-start.3
  36.1 1.9 %collective-permute-start.4 = (bf16[128,4096]{1,0:T(8,128)(2,1)}, bf16[128,4096]{1,0:T(8,128)(2,1)S(1)}, u32[]{:S(2)}, u32[]{:S(2)}) collective-permute-start(bf16[128,4096]{1,0:T(8,128)(2,1)} %collective-permute-done.refs_1_), channel_id=1, source_target_pairs={{0,32},{32,64},{64,96},{96,128},{128,160},{160,192},{192,224},{224... | collective-permute-start | bytes 3145736 | tf_op jit(solution)/shard_map/ppermute | solution.py:255
  38.0 2.2 %collective-permute-start.5 = (bf16[128,4096]{1,0:T(8,128)(2,1)}, bf16[128,4096]{1,0:T(8,128)(2,1)}, u32[]{:S(2)}, u32[]{:S(2)}) collective-permute-start(bf16[128,4096]{1,0:T(8,128)(2,1)} %collective-permute-done.1.refs_2_), channel_id=1, source_target_pairs={{0,224},{32,0},{64,32},{96,64},{128,96},{160,128},{192,160},{224,1... | collective-permute-start | bytes 3145736 | tf_op jit(solution)/shard_map/ppermute | solution.py:255
  40.3 1.7 shard_map.114
  42.0 4.4 %all-to-all-start.1 = ((bf16[16,256,128]{2,1,0:T(8,128)(2,1)}), bf16[16,256,128]{2,1,0:T(8,128)(2,1)S(1)}, u32[]{:S(2)}, u32[]{:S(2)}) async-start(bf16[16,256,128]{2,1,0:T(8,128)(2,1)} %shard_map.114), calls=%async_computation.1 | async-start | bytes 2097152 | tf_op jit(solution)/shard_map/all_to_all | solution.py:289
  46.4 17.5 %collective-permute-done.4.refs_3_ = bf16[128,4096]{1,0:T(8,128)(2,1)S(1)} collective-permute-done((bf16[128,4096]{1,0:T(8,128)(2,1)}, bf16[128,4096]{1,0:T(8,128)(2,1)S(1)}, u32[]{:S(2)}, u32[]{:S(2)}) %collective-permute-start.4) | collective-permute-done | bytes 1048608 | tf_op jit(solution)/shard_map/ppermute | solution.py:255
  63.9 0.7 collective-permute-done.5.refs_4_
  64.6 0.1 reduce_sum.30
  64.8 0.9 broadcast_in_dim.7
  65.6 8.1 %all-to-all-start.2 = ((bf16[8,256,128]{2,1,0:T(8,128)(2,1)}), bf16[8,256,128]{2,1,0:T(8,128)(2,1)S(1)}, u32[]{:S(2)}, u32[]{:S(2)}) async-start(bf16[8,256,128]{2,1,0:T(8,128)(2,1)} %broadcast_in_dim.7), calls=%async_computation.2 | async-start | bytes 1048576 | tf_op jit(solution)/shard_map/all_to_all | solution.py:231
  73.7 0.6 slice.44
  75.0 1.5 collective-permute-start.6
  76.5 0.6 collective-permute-start.7
  77.1 13.4 %all-to-all-done.2.emb_ref = bf16[8,256,128]{2,1,0:T(8,128)(2,1)S(1)} async-done(((bf16[8,256,128]{2,1,0:T(8,128)(2,1)}), bf16[8,256,128]{2,1,0:T(8,128)(2,1)S(1)}, u32[]{:S(2)}, u32[]{:S(2)}) %all-to-all-start.2) | async-done | bytes 524320 | tf_op jit(solution)/shard_map/all_to_all | solution.py:231
  90.5 4.3 %shard_map.115 = bf16[16,256,128]{2,1,0:T(8,128)(2,1)} custom-call(f32[16,8,256]{2,1,0:T(8,128)S(1)} %concatenate.79.ids_ref, bf16[8,256,128]{2,1,0:T(8,128)(2,1)S(1)} %all-to-all-done.2.emb_ref), custom_call_target="tpu_custom_call" | custom-call | flops 2147483648 | bytes 3145728 | tf_op jit(solution)/shard_map/pallas_call | solution.py:28
  94.9 4.5 %all-to-all-start.3 = ((bf16[16,256,128]{2,1,0:T(8,128)(2,1)}), bf16[16,256,128]{2,1,0:T(8,128)(2,1)}, u32[]{:S(2)}, u32[]{:S(2)}) async-start(bf16[16,256,128]{2,1,0:T(8,128)(2,1)} %shard_map.115), calls=%async_computation.3 | async-start | bytes 2097152 | tf_op jit(solution)/shard_map/all_to_all | solution.py:298
  99.5 0.2 copy.23
  99.7 1.3 add_subtract_fusion.next_ref
  101.2 4.4 %shard_map.116 = bf16[16,384,128]{2,1,0:T(8,128)(2,1)S(1)} custom-call(f32[16,8,384]{2,1,0:T(8,128)S(1)} %concatenate.80.ids_ref, bf16[8,256,128]{2,1,0:T(8,128)(2,1)S(1)} %all-to-all-done.2.emb_ref), custom_call_target="tpu_custom_call" | custom-call | flops 3221225472 | bytes 4718592 | tf_op jit(solution)/shard_map/pallas_call | solution.py:28
  105.6 1.1 copy-done.6
  106.7 0.5 collective-permute-done.6.refs_5_
  107.2 0.8 slice.49
  108.1 1.1 copy-done.4
  109.1 2.0 %slice.50 = bf16[64,4096]{1,0:T(8,128)(2,1)} slice(bf16[128,4096]{1,0:T(8,128)(2,1)} %collective-permute-done.7.refs_6_), slice={[64:128], [0:4096]} | slice | bytes 1048576 | tf_op jit(solution)/shard_map/slice | solution.py:308
  111.1 1.1 all-to-all-done.3.tokens_ref.token_ref
  112.3 0.4 collective-permute-start.16
  112.7 2.4 %collective-permute-start.17 = (bf16[64,4096]{1,0:T(8,128)(2,1)}, bf16[64,4096]{1,0:T(8,128)(2,1)}, u32[]{:S(2)}, u32[]{:S(2)}) collective-permute-start(bf16[64,4096]{1,0:T(8,128)(2,1)} %slice.50), channel_id=1, source_target_pairs={{0,224},{32,0},{64,32},{96,64},{128,96},{160,128},{192,160},{224,1... | collective-permute-start | bytes 1572872 | tf_op jit(solution)/shard_map/ppermute | solution.py:312
  115.1 4.7 %all-to-all-start.4 = ((bf16[16,384,128]{2,1,0:T(8,128)(2,1)}), bf16[16,384,128]{2,1,0:T(8,128)(2,1)}, u32[]{:S(2)}, u32[]{:S(2)}) async-start(bf16[16,384,128]{2,1,0:T(8,128)(2,1)} %copy-done.6), calls=%async_computation.4 | async-start | bytes 3145728 | tf_op jit(solution)/shard_map/all_to_all | solution.py:314
  119.8 1.9 %shard_map.117.part_ref = f32[256,384]{1,0:T(8,128)S(1)} custom-call(s32[1]{0:T(128)} %bitcast.tp_ref.half_ref, bf16[16,256,128]{2,1,0:T(8,128)(2,1)} %all-to-all-done.3.tokens_ref.token_ref, bf16[3,4096,128]{2,1,0:T(8,128)(2,1)S(1)} %bitcast.17), custom_call_target="tpu_custom_call" | custom-call | flops 402653184 | bytes 1572864 | tf_op jit(solution)/shard_map/pallas_call | solution.py:28
  121.8 2.6 %shard_map.118.refs_0_ = bf16[256,128]{1,0:T(8,128)(2,1)S(1)} custom-call(s32[1]{0:T(128)S(6)} %sub.38.half_ref, bf16[16,256,128]{2,1,0:T(8,128)(2,1)} %collective-permute-done.8.tokens_ref, bf16[3,4096,128]{2,1,0:T(8,128)(2,1)S(1)} %bitcast.18, f32[256,384]{1,0:T(8,128)S(1)} %shard_map.117.part_ref, f32[256,256]{1,0:T(8,128)S(1)} %fusion.1.allowed_ref), custom_call_target="tpu_custom_call" | custom-call | flops 402653184 | bytes 1572864 | tf_op jit(solution)/shard_map/pallas_call | solution.py:28
  124.4 3.0 %collective-permute-start.10 = (bf16[256,128]{1,0:T(8,128)(2,1)S(1)}, bf16[256,128]{1,0:T(8,128)(2,1)S(1)}, u32[]{:S(2)}, u32[]{:S(2)}) collective-permute-start(bf16[256,128]{1,0:T(8,128)(2,1)S(1)} %shard_map.118.refs_0_), channel_id=1, source_target_pairs={{0,224},{32,0},{64,32},{96,64},{128,96},{160,128},{192,160},{224,1... | collective-permute-start | bytes 196616 | tf_op jit(solution)/shard_map/ppermute | solution.py:335
  127.4 4.1 %collective-permute-start.12 = (bf16[256,128]{1,0:T(8,128)(2,1)S(1)}, bf16[256,128]{1,0:T(8,128)(2,1)S(1)}, u32[]{:S(2)}, u32[]{:S(2)}) collective-permute-start(bf16[256,128]{1,0:T(8,128)(2,1)S(1)} %shard_map.118.refs_0_), channel_id=1, source_target_pairs={{0,192},{32,224},{64,0},{96,32},{128,64},{160,96},{192,128},{224,1... | collective-permute-start | bytes 196616 | tf_op jit(solution)/shard_map/ppermute | solution.py:335
  131.5 0.8 collective-permute-start.13
  132.4 4.2 %collective-permute-start.14 = (bf16[256,128]{1,0:T(8,128)(2,1)S(1)}, bf16[256,128]{1,0:T(8,128)(2,1)S(1)}, u32[]{:S(2)}, u32[]{:S(2)}) collective-permute-start(bf16[256,128]{1,0:T(8,128)(2,1)S(1)} %shard_map.118.refs_0_), channel_id=1, source_target_pairs={{0,160},{32,192},{64,224},{96,0},{128,32},{160,64},{192,96},{224,1... | collective-permute-start | bytes 196616 | tf_op jit(solution)/shard_map/ppermute | solution.py:335
  136.6 2.2 %collective-permute-start.15 = (bf16[256,128]{1,0:T(8,128)(2,1)S(1)}, bf16[256,128]{1,0:T(8,128)(2,1)S(1)}, u32[]{:S(2)}, u32[]{:S(2)}) collective-permute-start(bf16[256,128]{1,0:T(8,128)(2,1)S(1)} %shard_map.118.refs_0_), channel_id=1, source_target_pairs={{0,128},{32,160},{64,192},{96,224},{128,0},{160,32},{192,64},{224,... | collective-permute-start | bytes 196616 | tf_op jit(solution)/shard_map/ppermute | solution.py:335
  138.8 2.7 %shard_map.119 = (bf16[1024,2048]{1,0:T(8,128)(2,1)S(1)}, bf16[1024,2048]{1,0:T(8,128)(2,1)S(1)}) custom-call(s32[1]{0:T(128)} %bitcast.tp_ref.half_ref, bf16[128,4096]{1,0:T(8,128)(2,1)S(1)} %copy-done.7, bf16[128,4096]{1,0:T(8,128)(2,1)} %collective-permute-done.refs_1_, bf16[128,4096]{1,0:T(8,128)(2,1)} %collective-permute-done.1.refs_2_, ...), custom_call_target="tpu_custom_call" | custom-call | bytes 16777216 | tf_op jit(solution)/shard_map/pallas_call | solution.py:28
  141.5 1.9 collective-permute-done.14.refs_6_
  143.4 1.4 collective-permute-done.15.refs_7_
  144.8 2.3 %shard_map.121 = bf16[256,2048]{1,0:T(8,128)(2,1)} custom-call(bf16[256,128]{1,0:T(8,128)(2,1)S(1)} %shard_map.118.refs_0_, bf16[256,128]{1,0:T(8,128)(2,1)S(1)} %collective-permute-done.9.refs_1_, bf16[256,128]{1,0:T(8,128)(2,1)S(1)} %collective-permute-done.10.refs_2_, bf16[256,128]{1,0:T(8,128)(2,1)S(1)} %collective-permute-done.11.refs_3_, ...), custom_call_target="tpu_custom_call" | custom-call | flops 1073741824 | bytes 4194304 | tf_op jit(solution)/shard_map/pallas_call | solution.py:28
  147.0 1.3 shard_map.120.own_ref
  148.3 1.6 collective-permute-done.18.got_ref
  149.9 1.0 copy-done.10
  150.9 1.2 copy-done.11
  152.1 2.7 %shard_map.122 = (bf16[256,2048]{1,0:T(8,128)(2,1)S(1)}, f32[256,512]{1,0:T(8,128)S(1)}) custom-call(f32[256,2048]{1,0:T(8,128)S(1)} %shard_map.120.own_ref, bf16[256,2048]{1,0:T(8,128)(2,1)S(1)} %copy-done.11, bf16[16,256,128]{2,1,0:T(8,128)(2,1)} %all-to-all-done.3.tokens_ref.token_ref, bf16[16,384,128]{2,1,0:T(8,128)(2,1)} %all-to-all-done.4.neg_ref), custom_call_target="tpu_custom_call" | custom-call | flops 402653184 | bytes 1572864 | tf_op jit(solution)/shard_map/pallas_call | solution.py:28
  154.8 0.2 collective-permute-start.19
  155.0 0.8 copy-done.12
  155.8 1.0 collective-permute-done.19.far_ref
  157.1 1.0 copy-done.13
  158.1 2.0 %shard_map.123 = (f32[8,128]{1,0:T(8,128)S(1)}, bf16[256,2048]{1,0:T(8,128)(2,1)}) custom-call(f32[256,512]{1,0:T(8,128)S(1)} %copy-done.13, f32[256,512]{1,0:T(8,128)S(1)} %collective-permute-done.19.far_ref, f32[256,1]{1,0:T(8,128)S(1)} %convert_element_type.25.usable_ref, s32[256,1]{1,0:T(8,128)S(1)} %copy-done.14, s32[384,1]{1,0:T(8,128)S(1)} %copy.25.slot_ref, ...), custom_call_target="tpu_custom_call" | custom-call | flops 268435456 | bytes 1048576 | tf_op jit(solution)/shard_map/pallas_call | solution.py:28
  160.1 7.1 %all-to-all-start.5 = ((bf16[16,16,2048]{2,1,0:T(8,128)(2,1)}), bf16[16,16,2048]{2,1,0:T(8,128)(2,1)S(1)}, u32[]{:S(2)}, u32[]{:S(2)}) async-start(bf16[16,16,2048]{2,1,0:T(8,128)(2,1)} %bitcast.8), calls=%async_computation.5 | async-start | bytes 2097152 | tf_op jit(solution)/shard_map/all_to_all | solution.py:385
  167.2 0.5 slice.45
  167.9 1.5 maximum_bitcast_fusion
  169.4 16.1 %all-to-all-done.5 = bf16[16,16,2048]{2,1,0:T(8,128)(2,1)S(1)} async-done(((bf16[16,16,2048]{2,1,0:T(8,128)(2,1)}), bf16[16,16,2048]{2,1,0:T(8,128)(2,1)S(1)}, u32[]{:S(2)}, u32[]{:S(2)}) %all-to-all-start.5) | async-done | bytes 1048608 | tf_op jit(solution)/shard_map/all_to_all | solution.py:385
  185.6 0.8 convert_reduce_fusion
  (74 shorter events, 1.8 us)
Async XLA Ops:
  0.6 28.9 %copy-start.2 = (bf16[4096,264]{0,1:T(8,128)(2,1)S(1)}, bf16[4096,264]{0,1:T(8,128)(2,1)}, u32[]{:S(2)}) copy-start(bf16[4096,264]{0,1:T(8,128)(2,1)} %param.10) | copy-start | bytes 6488068
  0.6 28.8 %collective-permute-start = (bf16[128,4096]{1,0:T(8,128)(2,1)}, bf16[128,4096]{1,0:T(8,128)(2,1)}, u32[]{:S(2)}, u32[]{:S(2)}) collective-permute-start(bf16[128,4096]{1,0:T(8,128)(2,1)} %refs_0_.1), channel_id=1, source_target_pairs={{0,32},{32,64},{64,96},{96,128},{128,160},{160,192},{192,224},{224... | collective-permute-start | bytes 3145736 | tf_op jit(solution)/shard_map/ppermute | solution.py:248
  2.6 26.8 %collective-permute-start.1 = (bf16[128,4096]{1,0:T(8,128)(2,1)}, bf16[128,4096]{1,0:T(8,128)(2,1)}, u32[]{:S(2)}, u32[]{:S(2)}) collective-permute-start(bf16[128,4096]{1,0:T(8,128)(2,1)} %refs_0_.1), channel_id=1, source_target_pairs={{0,224},{32,0},{64,32},{96,64},{128,96},{160,128},{192,160},{224,1... | collective-permute-start | bytes 3145736 | tf_op jit(solution)/shard_map/ppermute | solution.py:248
  29.5 2.9 %collective-permute-start.2 = (bf16[16,272,128]{2,1,0:T(8,128)(2,1)S(1)}, bf16[16,272,128]{2,1,0:T(8,128)(2,1)}, u32[]{:S(2)}, u32[]{:S(2)}) collective-permute-start(bf16[16,272,128]{2,1,0:T(8,128)(2,1)S(1)} %all_to_all.30.mine_ref), channel_id=1, source_target_pairs={{0,1},{1,0},{2,3},{3,2},{4,5},{5,4},{6,7},{7,6},{8,9},{9,8},{10,11... | collective-permute-start | bytes 3342344 | tf_op jit(solution)/shard_map/ppermute | solution.py:226
  29.5 1.6 copy-start.3
  31.1 1.6 copy-start.1
  35.5 4.7 %collective-permute-start.3 = (bf16[16,256,128]{2,1,0:T(8,128)(2,1)S(1)}, bf16[16,256,128]{2,1,0:T(8,128)(2,1)S(1)}, u32[]{:S(2)}, u32[]{:S(2)}) collective-permute-start(bf16[16,256,128]{2,1,0:T(8,128)(2,1)S(1)} %get-tuple-element.37), channel_id=1, source_target_pairs={{0,1},{1,0},{2,3},{3,2},{4,5},{5,4},{6,7},{7,6},{8,9},{9,8},{10,11... | collective-permute-start | bytes 3145736 | tf_op jit(solution)/shard_map/ppermute | solution.py:226
  36.1 27.8 %collective-permute-start.4 = (bf16[128,4096]{1,0:T(8,128)(2,1)}, bf16[128,4096]{1,0:T(8,128)(2,1)S(1)}, u32[]{:S(2)}, u32[]{:S(2)}) collective-permute-start(bf16[128,4096]{1,0:T(8,128)(2,1)} %collective-permute-done.refs_1_), channel_id=1, source_target_pairs={{0,32},{32,64},{64,96},{96,128},{128,160},{160,192},{192,224},{224... | collective-permute-start | bytes 3145736 | tf_op jit(solution)/shard_map/ppermute | solution.py:255
  38.0 26.6 %collective-permute-start.5 = (bf16[128,4096]{1,0:T(8,128)(2,1)}, bf16[128,4096]{1,0:T(8,128)(2,1)}, u32[]{:S(2)}, u32[]{:S(2)}) collective-permute-start(bf16[128,4096]{1,0:T(8,128)(2,1)} %collective-permute-done.1.refs_2_), channel_id=1, source_target_pairs={{0,224},{32,0},{64,32},{96,64},{128,96},{160,128},{192,160},{224,1... | collective-permute-start | bytes 3145736 | tf_op jit(solution)/shard_map/ppermute | solution.py:255
  42.0 31.7 %copy-start.15 = (s32[1,256]{1,0:T(1,128)S(1)}, s32[1,256]{1,0:T(1,128)}, u32[]{:S(2)}) copy-start(s32[1,256]{1,0:T(1,128)} %param.15) | copy-start | bytes 3076
  42.0 32.5 %copy-start.16 = (s32[1,16]{1,0:T(1,128)S(1)}, s32[1,16]{1,0:T(1,128)}, u32[]{:S(2)}) copy-start(s32[1,16]{1,0:T(1,128)} %param.16) | copy-start | bytes 196
  42.0 22.7 %all-to-all-start.1 = ((bf16[16,256,128]{2,1,0:T(8,128)(2,1)}), bf16[16,256,128]{2,1,0:T(8,128)(2,1)S(1)}, u32[]{:S(2)}, u32[]{:S(2)}) async-start(bf16[16,256,128]{2,1,0:T(8,128)(2,1)} %shard_map.114), calls=%async_computation.1 | async-start | bytes 2097152 | tf_op jit(solution)/shard_map/all_to_all | solution.py:289
  63.9 31.0 %copy-start.8 = (bf16[128,4096]{1,0:T(8,128)(2,1)}, bf16[128,4096]{1,0:T(8,128)(2,1)S(1)}, u32[]{:S(2)}) copy-start(bf16[128,4096]{1,0:T(8,128)(2,1)S(1)} %collective-permute-done.4.refs_3_) | copy-start | bytes 3145732
  65.6 24.9 %all-to-all-start.2 = ((bf16[8,256,128]{2,1,0:T(8,128)(2,1)}), bf16[8,256,128]{2,1,0:T(8,128)(2,1)S(1)}, u32[]{:S(2)}, u32[]{:S(2)}) async-start(bf16[8,256,128]{2,1,0:T(8,128)(2,1)} %broadcast_in_dim.7), calls=%async_computation.2 | async-start | bytes 1048576 | tf_op jit(solution)/shard_map/all_to_all | solution.py:231
  75.0 32.2 %collective-permute-start.6 = (bf16[128,4096]{1,0:T(8,128)(2,1)S(1)}, bf16[128,4096]{1,0:T(8,128)(2,1)S(1)}, u32[]{:S(2)}, u32[]{:S(2)}) collective-permute-start(bf16[128,4096]{1,0:T(8,128)(2,1)S(1)} %collective-permute-done.4.refs_3_), channel_id=1, source_target_pairs={{0,32},{32,64},{64,96},{96,128},{128,160},{160,192},{192,224},{224... | collective-permute-start | bytes 3145736 | tf_op jit(solution)/shard_map/ppermute | solution.py:291
  76.5 32.6 %collective-permute-start.7 = (bf16[128,4096]{1,0:T(8,128)(2,1)}, bf16[128,4096]{1,0:T(8,128)(2,1)}, u32[]{:S(2)}, u32[]{:S(2)}) collective-permute-start(bf16[128,4096]{1,0:T(8,128)(2,1)} %collective-permute-done.5.refs_4_), channel_id=1, source_target_pairs={{0,224},{32,0},{64,32},{96,64},{128,96},{160,128},{192,160},{224,1... | collective-permute-start | bytes 3145736 | tf_op jit(solution)/shard_map/ppermute | solution.py:291
  94.9 17.4 %all-to-all-start.3 = ((bf16[16,256,128]{2,1,0:T(8,128)(2,1)}), bf16[16,256,128]{2,1,0:T(8,128)(2,1)}, u32[]{:S(2)}, u32[]{:S(2)}) async-start(bf16[16,256,128]{2,1,0:T(8,128)(2,1)} %shard_map.115), calls=%async_computation.3 | async-start | bytes 2097152 | tf_op jit(solution)/shard_map/all_to_all | solution.py:298
  105.6 1.1 copy-start.6
  108.1 1.1 copy-start.4
  109.1 10.7 %copy-start = (bf16[4096,3,128]{2,0,1:T(8,128)(2,1)S(1)}, bf16[4096,3,128]{2,0,1:T(8,128)(2,1)}, u32[]{:S(2)}) copy-start(bf16[4096,3,128]{2,0,1:T(8,128)(2,1)} %param.13) | copy-start | bytes 9437188
  112.3 9.5 %collective-permute-start.8 = (bf16[16,256,128]{2,1,0:T(8,128)(2,1)}, bf16[16,256,128]{2,1,0:T(8,128)(2,1)}, u32[]{:S(2)}, u32[]{:S(2)}) collective-permute-start(bf16[16,256,128]{2,1,0:T(8,128)(2,1)} %all-to-all-done.3.tokens_ref.token_ref), channel_id=1, source_target_pairs={{0,1},{1,0},{2,3},{3,2},{4,5},{5,4},{6,7},{7,6},{8,9},{9,8},{10,11... | collective-permute-start | bytes 3145736 | tf_op jit(solution)/shard_map/ppermute | solution.py:226
  112.3 19.3 %collective-permute-start.16 = (bf16[64,4096]{1,0:T(8,128)(2,1)}, bf16[64,4096]{1,0:T(8,128)(2,1)}, u32[]{:S(2)}, u32[]{:S(2)}) collective-permute-start(bf16[64,4096]{1,0:T(8,128)(2,1)} %slice.49), channel_id=1, source_target_pairs={{0,32},{32,64},{64,96},{96,128},{128,160},{160,192},{192,224},{224... | collective-permute-start | bytes 1572872 | tf_op jit(solution)/shard_map/ppermute | solution.py:312
  112.7 19.6 %collective-permute-start.17 = (bf16[64,4096]{1,0:T(8,128)(2,1)}, bf16[64,4096]{1,0:T(8,128)(2,1)}, u32[]{:S(2)}, u32[]{:S(2)}) collective-permute-start(bf16[64,4096]{1,0:T(8,128)(2,1)} %slice.50), channel_id=1, source_target_pairs={{0,224},{32,0},{64,32},{96,64},{128,96},{160,128},{192,160},{224,1... | collective-permute-start | bytes 1572872 | tf_op jit(solution)/shard_map/ppermute | solution.py:312
  115.1 33.2 %all-to-all-start.4 = ((bf16[16,384,128]{2,1,0:T(8,128)(2,1)}), bf16[16,384,128]{2,1,0:T(8,128)(2,1)}, u32[]{:S(2)}, u32[]{:S(2)}) async-start(bf16[16,384,128]{2,1,0:T(8,128)(2,1)} %copy-done.6), calls=%async_computation.4 | async-start | bytes 3145728 | tf_op jit(solution)/shard_map/all_to_all | solution.py:314
  121.8 17.0 %copy-start.5 = (bf16[128,4096]{1,0:T(8,128)(2,1)S(1)}, bf16[128,4096]{1,0:T(8,128)(2,1)}, u32[]{:S(2)}) copy-start(bf16[128,4096]{1,0:T(8,128)(2,1)} %copy-done.4) | copy-start | bytes 3145732
  121.8 17.0 %copy-start.7 = (bf16[128,4096]{1,0:T(8,128)(2,1)S(1)}, bf16[128,4096]{1,0:T(8,128)(2,1)}, u32[]{:S(2)}) copy-start(bf16[128,4096]{1,0:T(8,128)(2,1)} %refs_0_.1) | copy-start | bytes 3145732
  121.8 17.0 %copy-start.9 = (bf16[128,4096]{1,0:T(8,128)(2,1)S(1)}, bf16[128,4096]{1,0:T(8,128)(2,1)}, u32[]{:S(2)}) copy-start(bf16[128,4096]{1,0:T(8,128)(2,1)} %copy-done.8) | copy-start | bytes 3145732
  124.4 12.2 %collective-permute-start.10 = (bf16[256,128]{1,0:T(8,128)(2,1)S(1)}, bf16[256,128]{1,0:T(8,128)(2,1)S(1)}, u32[]{:S(2)}, u32[]{:S(2)}) collective-permute-start(bf16[256,128]{1,0:T(8,128)(2,1)S(1)} %shard_map.118.refs_0_), channel_id=1, source_target_pairs={{0,224},{32,0},{64,32},{96,64},{128,96},{160,128},{192,160},{224,1... | collective-permute-start | bytes 196616 | tf_op jit(solution)/shard_map/ppermute | solution.py:335
  127.4 11.4 %collective-permute-start.11 = (bf16[256,128]{1,0:T(8,128)(2,1)S(1)}, bf16[256,128]{1,0:T(8,128)(2,1)S(1)}, u32[]{:S(2)}, u32[]{:S(2)}) collective-permute-start(bf16[256,128]{1,0:T(8,128)(2,1)S(1)} %shard_map.118.refs_0_), channel_id=1, source_target_pairs={{0,64},{32,96},{64,128},{96,160},{128,192},{160,224},{192,0},{224,... | collective-permute-start | bytes 196616 | tf_op jit(solution)/shard_map/ppermute | solution.py:335
  127.4 14.1 %collective-permute-start.12 = (bf16[256,128]{1,0:T(8,128)(2,1)S(1)}, bf16[256,128]{1,0:T(8,128)(2,1)S(1)}, u32[]{:S(2)}, u32[]{:S(2)}) collective-permute-start(bf16[256,128]{1,0:T(8,128)(2,1)S(1)} %shard_map.118.refs_0_), channel_id=1, source_target_pairs={{0,192},{32,224},{64,0},{96,32},{128,64},{160,96},{192,128},{224,1... | collective-permute-start | bytes 196616 | tf_op jit(solution)/shard_map/ppermute | solution.py:335
  131.5 10.0 %collective-permute-start.13 = (bf16[256,128]{1,0:T(8,128)(2,1)S(1)}, bf16[256,128]{1,0:T(8,128)(2,1)S(1)}, u32[]{:S(2)}, u32[]{:S(2)}) collective-permute-start(bf16[256,128]{1,0:T(8,128)(2,1)S(1)} %shard_map.118.refs_0_), channel_id=1, source_target_pairs={{0,96},{32,128},{64,160},{96,192},{128,224},{160,0},{192,32},{224,... | collective-permute-start | bytes 196616 | tf_op jit(solution)/shard_map/ppermute | solution.py:335
  132.4 11.0 %collective-permute-start.14 = (bf16[256,128]{1,0:T(8,128)(2,1)S(1)}, bf16[256,128]{1,0:T(8,128)(2,1)S(1)}, u32[]{:S(2)}, u32[]{:S(2)}) collective-permute-start(bf16[256,128]{1,0:T(8,128)(2,1)S(1)} %shard_map.118.refs_0_), channel_id=1, source_target_pairs={{0,160},{32,192},{64,224},{96,0},{128,32},{160,64},{192,96},{224,1... | collective-permute-start | bytes 196616 | tf_op jit(solution)/shard_map/ppermute | solution.py:335
  136.6 8.2 %collective-permute-start.15 = (bf16[256,128]{1,0:T(8,128)(2,1)S(1)}, bf16[256,128]{1,0:T(8,128)(2,1)S(1)}, u32[]{:S(2)}, u32[]{:S(2)}) collective-permute-start(bf16[256,128]{1,0:T(8,128)(2,1)S(1)} %shard_map.118.refs_0_), channel_id=1, source_target_pairs={{0,128},{32,160},{64,192},{96,224},{128,0},{160,32},{192,64},{224,... | collective-permute-start | bytes 196616 | tf_op jit(solution)/shard_map/ppermute | solution.py:335
  138.8 6.0 %collective-permute-start.9 = (bf16[256,128]{1,0:T(8,128)(2,1)S(1)}, bf16[256,128]{1,0:T(8,128)(2,1)S(1)}, u32[]{:S(2)}, u32[]{:S(2)}) collective-permute-start(bf16[256,128]{1,0:T(8,128)(2,1)S(1)} %shard_map.118.refs_0_), channel_id=1, source_target_pairs={{0,32},{32,64},{64,96},{96,128},{128,160},{160,192},{192,224},{224... | collective-permute-start | bytes 196616 | tf_op jit(solution)/shard_map/ppermute | solution.py:335
  147.0 2.9 %collective-permute-start.18 = (bf16[256,2048]{1,0:T(8,128)(2,1)}, bf16[256,2048]{1,0:T(8,128)(2,1)S(1)}, u32[]{:S(2)}, u32[]{:S(2)}) collective-permute-start(bf16[256,2048]{1,0:T(8,128)(2,1)} %shard_map.121), channel_id=1, source_target_pairs={{0,1},{1,0},{2,3},{3,2},{4,5},{5,4},{6,7},{7,6},{8,9},{9,8},{10,11... | collective-permute-start | bytes 3145736 | tf_op jit(solution)/shard_map/ppermute | solution.py:226
  147.0 10.0 %copy-start.14 = (s32[256,1]{1,0:T(8,128)S(1)}, s32[256,1]{1,0:T(8,128)}, u32[]{:S(2)}) copy-start(s32[256,1]{1,0:T(8,128)} %add_subtract_fusion.next_ref) | copy-start | bytes 3076
  149.9 1.0 copy-start.10
  150.9 1.2 copy-start.11
  154.8 2.0 %collective-permute-start.19 = (f32[256,512]{1,0:T(8,128)S(1)}, f32[256,512]{1,0:T(8,128)S(1)}, u32[]{:S(2)}, u32[]{:S(2)}) collective-permute-start(f32[256,512]{1,0:T(8,128)S(1)} %get-tuple-element.52.near_ref), channel_id=1, source_target_pairs={{0,1},{1,0},{2,3},{3,2},{4,5},{5,4},{6,7},{7,6},{8,9},{9,8},{10,11... | collective-permute-start | bytes 1572872 | tf_op jit(solution)/shard_map/ppermute | solution.py:226
  155.0 0.8 copy-start.12
  156.8 11.0 %collective-permute-start.20 = (bf16[256,2048]{1,0:T(8,128)(2,1)S(1)}, bf16[256,2048]{1,0:T(8,128)(2,1)S(1)}, u32[]{:S(2)}, u32[]{:S(2)}) collective-permute-start(bf16[256,2048]{1,0:T(8,128)(2,1)S(1)} %get-tuple-element.60.user_ref), channel_id=1, source_target_pairs={{0,1},{1,0},{2,3},{3,2},{4,5},{5,4},{6,7},{7,6},{8,9},{9,8},{10,11... | collective-permute-start | bytes 3145736 | tf_op jit(solution)/shard_map/ppermute | solution.py:226
  157.0 1.0 copy-start.13
  160.1 25.4 %all-to-all-start.5 = ((bf16[16,16,2048]{2,1,0:T(8,128)(2,1)}), bf16[16,16,2048]{2,1,0:T(8,128)(2,1)S(1)}, u32[]{:S(2)}, u32[]{:S(2)}) async-start(bf16[16,16,2048]{2,1,0:T(8,128)(2,1)} %bitcast.8), calls=%async_computation.5 | async-start | bytes 2097152 | tf_op jit(solution)/shard_map/all_to_all | solution.py:385
where the time goes:
time: 187 us; the launch traced here: 186 us
  waiting for transfers between devices  55.7 us (30%)
  starting transfers between devices  55.3 us (30%)
  Pallas kernels  29.4 us (16%)
  blocking collectives  24.3 us (13%)
  local copies, waits for them, and re-layouts  14.6 us (8%)
  other arithmetic  6.07 us (3%)
    pallas_call x12, Pallas kernels, call(): pl.pallas_call(kernel, out_shape=out_shape, in_specs=in_specs, out_specs=...  29.4 us
    all_to_all x1, blocking collectives, spread(): return lax.all_to_all(copies, axis, 0, 0, tiled=True)  24.3 us
    ppermute x4, waiting for transfers between devices, body(): pieces += [right(pieces[-2]), left(pieces[-1])]  18.7 us
    all_to_all x1, waiting for transfers between devices, body(): lax.all_to_all(item_part.reshape(users, row_count // users, half), 'user'...  16.1 us
    ppermute x7, starting transfers between devices, body(): lax.ppermute(attended, 'item', ring(shards, k))  14.4 us
    all_to_all x1, waiting for transfers between devices, spread(): return lax.all_to_all(copies, axis, 0, 0, tiled=True)  13.4 us
    unnamed x36, local copies, waits for them, and re-layouts  8.92 us
    all_to_all x1, starting transfers between devices, spread(): return lax.all_to_all(copies, axis, 0, 0, tiled=True)  8.07 us
  transfers between devices with their start and end apart: 26, of which 11 were waited for; matrix products, arithmetic and copies ran while one was open for 6% of the time, Pallas kernels for 13%

commit v1 on v0

--- a/solution.py
+++ b/solution.py
@@ -311,7 +311,6 @@
     allowed, usable, next_slot, neg_slot = masks
     far = [right(ends[0]), left(ends[1])]
     other_tokens = exchange(tokens)
-    negatives = lax.all_to_all(picked_negatives, "user", 0, 0, tiled=True)
 
     qkv = w_qkv.transpose(1, 0, 2)
     qkv_width = qkv.shape[0] * qkv.shape[2]
@@ -331,6 +330,8 @@
         flops=seq_steps * D * qkv_width,
         moved=D * qkv_width,
     )
+    attended, picked_negatives = lax.optimization_barrier((attended, picked_negatives))
+    negatives = lax.all_to_all(picked_negatives, "user", 0, 0, tiled=True)
     shifts = [0, 1, -1, 2, -2, 3, -3, 4]
     heads = [attended] + [lax.ppermute(attended, "item", ring(shards, k)) for k in shifts[1:]]
     w_send, w_keep = call(
@@ -354,6 +355,7 @@
 
     got_user = exchange(mixed(w_send, bf16))
     own_user = mixed(w_keep, f32)
+    own_user, got_user = lax.optimization_barrier((own_user, got_user))
     user_half, near = call(
         user_kernel,
         (

time: 187 us -> 186 us (level)
  waiting for transfers between devices: 55.7 us -> 52.6 us
  Pallas kernels: 29.4 us -> 27.5 us
  other arithmetic: 6.07 us -> 7.95 us
    pallas_call x12, Pallas kernels: 29.4 us -> 27.5 us  [call(): pl.pallas_call(kernel, out_shape=out_shape, in_specs=in_specs, out_specs=...]
    unnamed x36 -> x34, local copies, waits for them, and re-layouts: 8.92 us -> 8.91 us
  transfers between devices with their start and end apart: 26 -> 26, of which waited for: 11 -> 10; matrix products, arithmetic and copies ran while one was open for 6% -> 7% of each run, Pallas kernels for 13% -> 12%
where the time goes in v1:
time: 186 us; the launch traced here: 185 us
  starting transfers between devices  55.8 us (30%)
  waiting for transfers between devices  52.6 us (28%)
  Pallas kernels  27.5 us (15%)
  blocking collectives  24.3 us (13%)
  local copies, waits for them, and re-layouts  15.5 us (8%)
  other arithmetic  7.95 us (4%)
    pallas_call x12, Pallas kernels, call(): pl.pallas_call(kernel, out_shape=out_shape, in_specs=in_specs, out_specs=...  27.5 us
    all_to_all x1, blocking collectives, spread(): return lax.all_to_all(copies, axis, 0, 0, tiled=True)  24.3 us
    ppermute x4, waiting for transfers between devices, body(): pieces += [right(pieces[-2]), left(pieces[-1])]  18.2 us
    all_to_all x1, waiting for transfers between devices, body(): lax.all_to_all(item_part.reshape(users, row_count // users, half), 'user'...  14.9 us
    all_to_all x1, waiting for transfers between devices, spread(): return lax.all_to_all(copies, axis, 0, 0, tiled=True)  13.4 us
    ppermute x7, starting transfers between devices, body(): lax.ppermute(attended, 'item', ring(shards, k))  13 us
    unnamed x34, local copies, waits for them, and re-layouts  8.91 us
    all_to_all x1, starting transfers between devices, spread(): return lax.all_to_all(copies, axis, 0, 0, tiled=True)  8.07 us
  transfers between devices with their start and end apart: 26, of which 10 were waited for; matrix products, arithmetic and copies ran while one was open for 7% of the time, Pallas kernels for 12%

profile of v1, /device:TPU:32, one launch (start us, length us, event | category | flops | bytes accessed | tf_op | source)
XLA Modules:
  0.0 184.5 jit_solution(5326047569434997396)
XLA Ops:
  0.6 2.0 %collective-permute-start = (bf16[128,4096]{1,0:T(8,128)(2,1)}, bf16[128,4096]{1,0:T(8,128)(2,1)}, u32[]{:S(2)}, u32[]{:S(2)}) collective-permute-start(bf16[128,4096]{1,0:T(8,128)(2,1)} %refs_0_.1), channel_id=1, source_target_pairs={{0,32},{32,64},{64,96},{96,128},{128,160},{160,192},{192,224},{224... | collective-permute-start | bytes 3145736 | tf_op jit(solution)/shard_map/ppermute | solution.py:248
  2.7 0.7 constant_dynamic-update-slice_fusion.1
  3.4 0.7 subtract_bitcast_fusion
  4.2 0.8 fusion.3
  5.2 24.3 %all_to_all.30.mine_ref = bf16[16,272,128]{2,1,0:T(8,128)(2,1)S(1)} all-to-all(bf16[16,272,128]{2,1,0:T(8,128)(2,1)S(1)} %broadcast_in_dim.6), channel_id=1, replica_groups=mesh['item'=8,'user'=16,'tp'=2] {'user'}, dimensions={0} | all-to-all | bytes 2228224 | tf_op jit(solution)/shard_map/all_to_all | solution.py:231
  29.5 1.6 copy-done.3
  31.1 0.8 shard_map.112
  31.9 0.4 collective-permute-done.2.other_ref
  32.4 0.4 copy-done.1
  32.7 2.8 %shard_map.113 = (bf16[256,264]{1,0:T(8,128)(2,1)S(1)}, bf16[16,256,128]{2,1,0:T(8,128)(2,1)S(1)}) custom-call(s32[1]{0:T(128)} %bitcast.tp_ref.half_ref, bf16[16,272,128]{2,1,0:T(8,128)(2,1)} %collective-permute-done.2.other_ref, f32[264,256]{1,0:T(8,128)S(1)} %get-tuple-element.38.gate_near, f32[264,256]{1,0:T(8,128)S(1)} %get-tuple-element.39.up_near, ...), custom_call_target="tpu_custom_call" | custom-call | flops 830472192 | bytes 6488064 | tf_op jit(solution)/shard_map/pallas_call | solution.py:28
  35.5 0.6 collective-permute-start.3
  36.1 1.9 %collective-permute-start.4 = (bf16[128,4096]{1,0:T(8,128)(2,1)}, bf16[128,4096]{1,0:T(8,128)(2,1)}, u32[]{:S(2)}, u32[]{:S(2)}) collective-permute-start(bf16[128,4096]{1,0:T(8,128)(2,1)} %collective-permute-done.refs_1_), channel_id=1, source_target_pairs={{0,32},{32,64},{64,96},{96,128},{128,160},{160,192},{192,224},{224... | collective-permute-start | bytes 3145736 | tf_op jit(solution)/shard_map/ppermute | solution.py:255
  38.0 2.2 %collective-permute-start.5 = (bf16[128,4096]{1,0:T(8,128)(2,1)}, bf16[128,4096]{1,0:T(8,128)(2,1)}, u32[]{:S(2)}, u32[]{:S(2)}) collective-permute-start(bf16[128,4096]{1,0:T(8,128)(2,1)} %collective-permute-done.1.refs_2_), channel_id=1, source_target_pairs={{0,224},{32,0},{64,32},{96,64},{128,96},{160,128},{192,160},{224,1... | collective-permute-start | bytes 3145736 | tf_op jit(solution)/shard_map/ppermute | solution.py:255
  40.3 1.7 shard_map.114
  42.0 4.4 %all-to-all-start.1 = ((bf16[16,256,128]{2,1,0:T(8,128)(2,1)}), bf16[16,256,128]{2,1,0:T(8,128)(2,1)S(1)}, u32[]{:S(2)}, u32[]{:S(2)}) async-start(bf16[16,256,128]{2,1,0:T(8,128)(2,1)} %shard_map.114), calls=%async_computation.1 | async-start | bytes 2097152 | tf_op jit(solution)/shard_map/all_to_all | solution.py:289
  46.4 17.6 %collective-permute-done.4.refs_3_ = bf16[128,4096]{1,0:T(8,128)(2,1)} collective-permute-done((bf16[128,4096]{1,0:T(8,128)(2,1)}, bf16[128,4096]{1,0:T(8,128)(2,1)}, u32[]{:S(2)}, u32[]{:S(2)}) %collective-permute-start.4) | collective-permute-done | bytes 1048608 | tf_op jit(solution)/shard_map/ppermute | solution.py:255
  64.0 0.6 collective-permute-done.5.refs_4_
  64.8 0.9 broadcast_in_dim.7
  65.6 8.1 %all-to-all-start.2 = ((bf16[8,256,128]{2,1,0:T(8,128)(2,1)}), bf16[8,256,128]{2,1,0:T(8,128)(2,1)S(1)}, u32[]{:S(2)}, u32[]{:S(2)}) async-start(bf16[8,256,128]{2,1,0:T(8,128)(2,1)} %broadcast_in_dim.7), calls=%async_computation.2 | async-start | bytes 1048576 | tf_op jit(solution)/shard_map/all_to_all | solution.py:231
  73.7 0.6 slice.44
  75.0 1.5 collective-permute-start.6
  76.5 0.6 collective-permute-start.7
  77.1 13.4 %all-to-all-done.2.emb_ref = bf16[8,256,128]{2,1,0:T(8,128)(2,1)S(1)} async-done(((bf16[8,256,128]{2,1,0:T(8,128)(2,1)}), bf16[8,256,128]{2,1,0:T(8,128)(2,1)S(1)}, u32[]{:S(2)}, u32[]{:S(2)}) %all-to-all-start.2) | async-done | bytes 524320 | tf_op jit(solution)/shard_map/all_to_all | solution.py:231
  90.5 4.3 %shard_map.115 = bf16[16,256,128]{2,1,0:T(8,128)(2,1)} custom-call(f32[16,8,256]{2,1,0:T(8,128)S(1)} %concatenate.79.ids_ref, bf16[8,256,128]{2,1,0:T(8,128)(2,1)S(1)} %all-to-all-done.2.emb_ref), custom_call_target="tpu_custom_call" | custom-call | flops 2147483648 | bytes 3145728 | tf_op jit(solution)/shard_map/pallas_call | solution.py:28
  94.8 4.5 %all-to-all-start.3 = ((bf16[16,256,128]{2,1,0:T(8,128)(2,1)}), bf16[16,256,128]{2,1,0:T(8,128)(2,1)}, u32[]{:S(2)}, u32[]{:S(2)}) async-start(bf16[16,256,128]{2,1,0:T(8,128)(2,1)} %shard_map.115), calls=%async_computation.3 | async-start | bytes 2097152 | tf_op jit(solution)/shard_map/all_to_all | solution.py:298
  99.5 0.2 copy.23
  99.7 0.7 convert_element_type.25.usable_ref
  100.4 1.3 add_subtract_fusion.next_ref
  101.9 1.0 copy-done.13
  102.9 4.4 %shard_map.116 = bf16[16,384,128]{2,1,0:T(8,128)(2,1)S(1)} custom-call(f32[16,8,384]{2,1,0:T(8,128)S(1)} %concatenate.80.ids_ref, bf16[8,256,128]{2,1,0:T(8,128)(2,1)S(1)} %copy-done.13), custom_call_target="tpu_custom_call" | custom-call | flops 3221225472 | bytes 4718592 | tf_op jit(solution)/shard_map/pallas_call | solution.py:28
  107.3 1.1 copy-done.4
  108.4 1.9 %slice.49 = bf16[64,4096]{1,0:T(8,128)(2,1)} slice(bf16[128,4096]{1,0:T(8,128)(2,1)} %collective-permute-done.6.refs_5_), slice={[0:64], [0:4096]} | slice | bytes 1048576 | tf_op jit(solution)/shard_map/slice | solution.py:308
  110.3 1.9 %slice.50 = bf16[64,4096]{1,0:T(8,128)(2,1)} slice(bf16[128,4096]{1,0:T(8,128)(2,1)} %collective-permute-done.7.refs_6_), slice={[64:128], [0:4096]} | slice | bytes 1048576 | tf_op jit(solution)/shard_map/slice | solution.py:308
  112.3 0.4 collective-permute-start.16
  112.7 2.4 %collective-permute-start.17 = (bf16[64,4096]{1,0:T(8,128)(2,1)}, bf16[64,4096]{1,0:T(8,128)(2,1)}, u32[]{:S(2)}, u32[]{:S(2)}) collective-permute-start(bf16[64,4096]{1,0:T(8,128)(2,1)} %slice.50), channel_id=1, source_target_pairs={{0,224},{32,0},{64,32},{96,64},{128,96},{160,128},{192,160},{224,1... | collective-permute-start | bytes 1572872 | tf_op jit(solution)/shard_map/ppermute | solution.py:312
  115.1 1.9 %shard_map.117.part_ref = f32[256,384]{1,0:T(8,128)S(1)} custom-call(s32[1]{0:T(128)} %bitcast.tp_ref.half_ref, bf16[16,256,128]{2,1,0:T(8,128)(2,1)} %all-to-all-done.3.tokens_ref.token_ref, bf16[3,4096,128]{2,1,0:T(8,128)(2,1)S(1)} %bitcast.17), custom_call_target="tpu_custom_call" | custom-call | flops 402653184 | bytes 1572864 | tf_op jit(solution)/shard_map/pallas_call | solution.py:28
  117.0 1.2 shard_map.118.refs_0_
  118.2 6.4 %all-to-all-start.4 = ((bf16[16,384,128]{2,1,0:T(8,128)(2,1)}), bf16[16,384,128]{2,1,0:T(8,128)(2,1)}, u32[]{:S(2)}, u32[]{:S(2)}) async-start(bf16[16,384,128]{2,1,0:T(8,128)(2,1)} %copy-done.4), calls=%async_computation.4 | async-start | bytes 3145728 | tf_op jit(solution)/shard_map/all_to_all | solution.py:334
  124.7 2.0 %collective-permute-start.10 = (bf16[256,128]{1,0:T(8,128)(2,1)S(1)}, bf16[256,128]{1,0:T(8,128)(2,1)S(1)}, u32[]{:S(2)}, u32[]{:S(2)}) collective-permute-start(bf16[256,128]{1,0:T(8,128)(2,1)S(1)} %shard_map.118.refs_0_), channel_id=1, source_target_pairs={{0,224},{32,0},{64,32},{96,64},{128,96},{160,128},{192,160},{224,1... | collective-permute-start | bytes 196616 | tf_op jit(solution)/shard_map/ppermute | solution.py:336
  126.7 4.1 %collective-permute-start.12 = (bf16[256,128]{1,0:T(8,128)(2,1)S(1)}, bf16[256,128]{1,0:T(8,128)(2,1)S(1)}, u32[]{:S(2)}, u32[]{:S(2)}) collective-permute-start(bf16[256,128]{1,0:T(8,128)(2,1)S(1)} %shard_map.118.refs_0_), channel_id=1, source_target_pairs={{0,192},{32,224},{64,0},{96,32},{128,64},{160,96},{192,128},{224,1... | collective-permute-start | bytes 196616 | tf_op jit(solution)/shard_map/ppermute | solution.py:336
  130.8 0.8 collective-permute-start.13
  131.7 4.2 %collective-permute-start.14 = (bf16[256,128]{1,0:T(8,128)(2,1)S(1)}, bf16[256,128]{1,0:T(8,128)(2,1)S(1)}, u32[]{:S(2)}, u32[]{:S(2)}) collective-permute-start(bf16[256,128]{1,0:T(8,128)(2,1)S(1)} %shard_map.118.refs_0_), channel_id=1, source_target_pairs={{0,160},{32,192},{64,224},{96,0},{128,32},{160,64},{192,96},{224,1... | collective-permute-start | bytes 196616 | tf_op jit(solution)/shard_map/ppermute | solution.py:336
  135.9 1.6 collective-permute-start.15
  137.5 0.2 collective-permute-start.9
  137.7 3.3 %shard_map.119 = (bf16[1024,2048]{1,0:T(8,128)(2,1)S(1)}, bf16[1024,2048]{1,0:T(8,128)(2,1)S(1)}) custom-call(s32[1]{0:T(128)} %bitcast.tp_ref.half_ref, bf16[128,4096]{1,0:T(8,128)(2,1)S(1)} %copy-done.5, bf16[128,4096]{1,0:T(8,128)(2,1)} %collective-permute-done.refs_1_, bf16[128,4096]{1,0:T(8,128)(2,1)} %collective-permute-done.1.refs_2_, ...), custom_call_target="tpu_custom_call" | custom-call | bytes 16777216 | tf_op jit(solution)/shard_map/pallas_call | solution.py:28
  141.0 2.0 %collective-permute-done.14.refs_6_ = bf16[256,128]{1,0:T(8,128)(2,1)S(1)} collective-permute-done((bf16[256,128]{1,0:T(8,128)(2,1)S(1)}, bf16[256,128]{1,0:T(8,128)(2,1)S(1)}, u32[]{:S(2)}, u32[]{:S(2)}) %collective-permute-start.14) | collective-permute-done | bytes 65568 | tf_op jit(solution)/shard_map/ppermute | solution.py:336
  142.9 1.1 collective-permute-done.15.refs_7_
  144.1 1.2 shard_map.121
  145.4 1.2 shard_map.120.own_ref
  146.7 1.4 collective-permute-done.18.got_ref
  148.1 1.0 copy-done.6
  149.0 1.2 copy-done.7
  150.3 2.7 %shard_map.122 = (bf16[256,2048]{1,0:T(8,128)(2,1)S(1)}, f32[256,512]{1,0:T(8,128)S(1)}) custom-call(f32[256,2048]{1,0:T(8,128)S(1)} %shard_map.120.own_ref, bf16[256,2048]{1,0:T(8,128)(2,1)S(1)} %copy-done.7, bf16[16,256,128]{2,1,0:T(8,128)(2,1)} %all-to-all-done.3.tokens_ref.token_ref, bf16[16,384,128]{2,1,0:T(8,128)(2,1)} %all-to-all-done.4.neg_ref), custom_call_target="tpu_custom_call" | custom-call | flops 402653184 | bytes 1572864 | tf_op jit(solution)/shard_map/pallas_call | solution.py:28
  152.9 0.2 collective-permute-start.19
  153.2 0.8 copy-done.8
  153.9 1.0 collective-permute-done.19.far_ref
  155.2 1.0 copy-done.9
  156.3 2.0 %shard_map.123 = (f32[8,128]{1,0:T(8,128)S(1)}, bf16[256,2048]{1,0:T(8,128)(2,1)}) custom-call(f32[256,512]{1,0:T(8,128)S(1)} %copy-done.9, f32[256,512]{1,0:T(8,128)S(1)} %collective-permute-done.19.far_ref, f32[256,1]{1,0:T(8,128)S(1)} %copy-done.10, s32[256,1]{1,0:T(8,128)S(1)} %copy-done.11, s32[384,1]{1,0:T(8,128)S(1)} %copy.25.slot_ref, ...), custom_call_target="tpu_custom_call" | custom-call | flops 268435456 | bytes 1048576 | tf_op jit(solution)/shard_map/pallas_call | solution.py:28
  158.3 7.1 %all-to-all-start.5 = ((bf16[16,16,2048]{2,1,0:T(8,128)(2,1)}), bf16[16,16,2048]{2,1,0:T(8,128)(2,1)S(1)}, u32[]{:S(2)}, u32[]{:S(2)}) async-start(bf16[16,16,2048]{2,1,0:T(8,128)(2,1)} %bitcast.8), calls=%async_computation.5 | async-start | bytes 2097152 | tf_op jit(solution)/shard_map/all_to_all | solution.py:387
  165.4 0.5 slice.45
  165.9 1.4 broadcast_select_fusion.1
  167.3 1.5 maximum_bitcast_fusion
  168.8 14.9 %all-to-all-done.5 = bf16[16,16,2048]{2,1,0:T(8,128)(2,1)S(1)} async-done(((bf16[16,16,2048]{2,1,0:T(8,128)(2,1)}), bf16[16,16,2048]{2,1,0:T(8,128)(2,1)S(1)}, u32[]{:S(2)}, u32[]{:S(2)}) %all-to-all-start.5) | async-done | bytes 1048608 | tf_op jit(solution)/shard_map/all_to_all | solution.py:387
  183.7 0.8 convert_reduce_fusion
  (72 shorter events, 2.0 us)
Async XLA Ops:
  0.6 28.9 %copy-start.2 = (bf16[4096,264]{0,1:T(8,128)(2,1)S(1)}, bf16[4096,264]{0,1:T(8,128)(2,1)}, u32[]{:S(2)}) copy-start(bf16[4096,264]{0,1:T(8,128)(2,1)} %param.10) | copy-start | bytes 6488068
  0.6 28.8 %collective-permute-start = (bf16[128,4096]{1,0:T(8,128)(2,1)}, bf16[128,4096]{1,0:T(8,128)(2,1)}, u32[]{:S(2)}, u32[]{:S(2)}) collective-permute-start(bf16[128,4096]{1,0:T(8,128)(2,1)} %refs_0_.1), channel_id=1, source_target_pairs={{0,32},{32,64},{64,96},{96,128},{128,160},{160,192},{192,224},{224... | collective-permute-start | bytes 3145736 | tf_op jit(solution)/shard_map/ppermute | solution.py:248
  2.6 26.8 %collective-permute-start.1 = (bf16[128,4096]{1,0:T(8,128)(2,1)}, bf16[128,4096]{1,0:T(8,128)(2,1)}, u32[]{:S(2)}, u32[]{:S(2)}) collective-permute-start(bf16[128,4096]{1,0:T(8,128)(2,1)} %refs_0_.1), channel_id=1, source_target_pairs={{0,224},{32,0},{64,32},{96,64},{128,96},{160,128},{192,160},{224,1... | collective-permute-start | bytes 3145736 | tf_op jit(solution)/shard_map/ppermute | solution.py:248
  29.5 2.9 %collective-permute-start.2 = (bf16[16,272,128]{2,1,0:T(8,128)(2,1)S(1)}, bf16[16,272,128]{2,1,0:T(8,128)(2,1)}, u32[]{:S(2)}, u32[]{:S(2)}) collective-permute-start(bf16[16,272,128]{2,1,0:T(8,128)(2,1)S(1)} %all_to_all.30.mine_ref), channel_id=1, source_target_pairs={{0,1},{1,0},{2,3},{3,2},{4,5},{5,4},{6,7},{7,6},{8,9},{9,8},{10,11... | collective-permute-start | bytes 3342344 | tf_op jit(solution)/shard_map/ppermute | solution.py:226
  29.5 1.6 copy-start.3
  31.1 1.6 copy-start.1
  35.5 4.7 %collective-permute-start.3 = (bf16[16,256,128]{2,1,0:T(8,128)(2,1)S(1)}, bf16[16,256,128]{2,1,0:T(8,128)(2,1)S(1)}, u32[]{:S(2)}, u32[]{:S(2)}) collective-permute-start(bf16[16,256,128]{2,1,0:T(8,128)(2,1)S(1)} %get-tuple-element.41), channel_id=1, source_target_pairs={{0,1},{1,0},{2,3},{3,2},{4,5},{5,4},{6,7},{7,6},{8,9},{9,8},{10,11... | collective-permute-start | bytes 3145736 | tf_op jit(solution)/shard_map/ppermute | solution.py:226
  36.1 27.9 %collective-permute-start.4 = (bf16[128,4096]{1,0:T(8,128)(2,1)}, bf16[128,4096]{1,0:T(8,128)(2,1)}, u32[]{:S(2)}, u32[]{:S(2)}) collective-permute-start(bf16[128,4096]{1,0:T(8,128)(2,1)} %collective-permute-done.refs_1_), channel_id=1, source_target_pairs={{0,32},{32,64},{64,96},{96,128},{128,160},{160,192},{192,224},{224... | collective-permute-start | bytes 3145736 | tf_op jit(solution)/shard_map/ppermute | solution.py:255
  38.0 26.6 %collective-permute-start.5 = (bf16[128,4096]{1,0:T(8,128)(2,1)}, bf16[128,4096]{1,0:T(8,128)(2,1)}, u32[]{:S(2)}, u32[]{:S(2)}) collective-permute-start(bf16[128,4096]{1,0:T(8,128)(2,1)} %collective-permute-done.1.refs_2_), channel_id=1, source_target_pairs={{0,224},{32,0},{64,32},{96,64},{128,96},{160,128},{192,160},{224,1... | collective-permute-start | bytes 3145736 | tf_op jit(solution)/shard_map/ppermute | solution.py:255
  42.0 31.8 %copy-start.14 = (s32[1,256]{1,0:T(1,128)S(1)}, s32[1,256]{1,0:T(1,128)}, u32[]{:S(2)}) copy-start(s32[1,256]{1,0:T(1,128)} %param.15) | copy-start | bytes 3076
  42.0 32.6 %copy-start.15 = (s32[1,16]{1,0:T(1,128)S(1)}, s32[1,16]{1,0:T(1,128)}, u32[]{:S(2)}) copy-start(s32[1,16]{1,0:T(1,128)} %param.16) | copy-start | bytes 196
  42.0 22.7 %all-to-all-start.1 = ((bf16[16,256,128]{2,1,0:T(8,128)(2,1)}), bf16[16,256,128]{2,1,0:T(8,128)(2,1)S(1)}, u32[]{:S(2)}, u32[]{:S(2)}) async-start(bf16[16,256,128]{2,1,0:T(8,128)(2,1)} %shard_map.114), calls=%async_computation.1 | async-start | bytes 2097152 | tf_op jit(solution)/shard_map/all_to_all | solution.py:289
  65.6 24.9 %all-to-all-start.2 = ((bf16[8,256,128]{2,1,0:T(8,128)(2,1)}), bf16[8,256,128]{2,1,0:T(8,128)(2,1)S(1)}, u32[]{:S(2)}, u32[]{:S(2)}) async-start(bf16[8,256,128]{2,1,0:T(8,128)(2,1)} %broadcast_in_dim.7), calls=%async_computation.2 | async-start | bytes 1048576 | tf_op jit(solution)/shard_map/all_to_all | solution.py:231
  75.0 33.4 %collective-permute-start.6 = (bf16[128,4096]{1,0:T(8,128)(2,1)}, bf16[128,4096]{1,0:T(8,128)(2,1)}, u32[]{:S(2)}, u32[]{:S(2)}) collective-permute-start(bf16[128,4096]{1,0:T(8,128)(2,1)} %collective-permute-done.4.refs_3_), channel_id=1, source_target_pairs={{0,32},{32,64},{64,96},{96,128},{128,160},{160,192},{192,224},{224... | collective-permute-start | bytes 3145736 | tf_op jit(solution)/shard_map/ppermute | solution.py:291
  76.5 33.8 %collective-permute-start.7 = (bf16[128,4096]{1,0:T(8,128)(2,1)}, bf16[128,4096]{1,0:T(8,128)(2,1)}, u32[]{:S(2)}, u32[]{:S(2)}) collective-permute-start(bf16[128,4096]{1,0:T(8,128)(2,1)} %collective-permute-done.5.refs_4_), channel_id=1, source_target_pairs={{0,224},{32,0},{64,32},{96,64},{128,96},{160,128},{192,160},{224,1... | collective-permute-start | bytes 3145736 | tf_op jit(solution)/shard_map/ppermute | solution.py:291
  90.5 4.3 %copy-start.12 = (bf16[8,256,128]{2,1,0:T(8,128)(2,1)}, bf16[8,256,128]{2,1,0:T(8,128)(2,1)S(1)}, u32[]{:S(2)}) copy-start(bf16[8,256,128]{2,1,0:T(8,128)(2,1)S(1)} %all-to-all-done.2.emb_ref) | copy-start | bytes 1572868
  94.8 17.4 %all-to-all-start.3 = ((bf16[16,256,128]{2,1,0:T(8,128)(2,1)}), bf16[16,256,128]{2,1,0:T(8,128)(2,1)}, u32[]{:S(2)}, u32[]{:S(2)}) async-start(bf16[16,256,128]{2,1,0:T(8,128)(2,1)} %shard_map.115), calls=%async_computation.3 | async-start | bytes 2097152 | tf_op jit(solution)/shard_map/all_to_all | solution.py:298
  101.9 1.0 copy-start.13
  102.9 12.2 %copy-start = (bf16[4096,3,128]{2,0,1:T(8,128)(2,1)S(1)}, bf16[4096,3,128]{2,0,1:T(8,128)(2,1)}, u32[]{:S(2)}) copy-start(bf16[4096,3,128]{2,0,1:T(8,128)(2,1)} %param.13) | copy-start | bytes 9437188
  107.3 1.1 copy-start.4
  112.3 4.7 %collective-permute-start.8 = (bf16[16,256,128]{2,1,0:T(8,128)(2,1)}, bf16[16,256,128]{2,1,0:T(8,128)(2,1)S(1)}, u32[]{:S(2)}, u32[]{:S(2)}) collective-permute-start(bf16[16,256,128]{2,1,0:T(8,128)(2,1)} %all-to-all-done.3.tokens_ref.token_ref), channel_id=1, source_target_pairs={{0,1},{1,0},{2,3},{3,2},{4,5},{5,4},{6,7},{7,6},{8,9},{9,8},{10,11... | collective-permute-start | bytes 3145736 | tf_op jit(solution)/shard_map/ppermute | solution.py:226
  112.3 18.6 %collective-permute-start.16 = (bf16[64,4096]{1,0:T(8,128)(2,1)}, bf16[64,4096]{1,0:T(8,128)(2,1)}, u32[]{:S(2)}, u32[]{:S(2)}) collective-permute-start(bf16[64,4096]{1,0:T(8,128)(2,1)} %slice.49), channel_id=1, source_target_pairs={{0,32},{32,64},{64,96},{96,128},{128,160},{160,192},{192,224},{224... | collective-permute-start | bytes 1572872 | tf_op jit(solution)/shard_map/ppermute | solution.py:312
  112.7 19.0 %collective-permute-start.17 = (bf16[64,4096]{1,0:T(8,128)(2,1)}, bf16[64,4096]{1,0:T(8,128)(2,1)}, u32[]{:S(2)}, u32[]{:S(2)}) collective-permute-start(bf16[64,4096]{1,0:T(8,128)(2,1)} %slice.50), channel_id=1, source_target_pairs={{0,224},{32,0},{64,32},{96,64},{128,96},{160,128},{192,160},{224,1... | collective-permute-start | bytes 1572872 | tf_op jit(solution)/shard_map/ppermute | solution.py:312
  118.2 19.5 %copy-start.5 = (bf16[128,4096]{1,0:T(8,128)(2,1)S(1)}, bf16[128,4096]{1,0:T(8,128)(2,1)}, u32[]{:S(2)}) copy-start(bf16[128,4096]{1,0:T(8,128)(2,1)} %refs_0_.1) | copy-start | bytes 3145732
  118.2 30.8 %all-to-all-start.4 = ((bf16[16,384,128]{2,1,0:T(8,128)(2,1)}), bf16[16,384,128]{2,1,0:T(8,128)(2,1)}, u32[]{:S(2)}, u32[]{:S(2)}) async-start(bf16[16,384,128]{2,1,0:T(8,128)(2,1)} %copy-done.4), calls=%async_computation.4 | async-start | bytes 3145728 | tf_op jit(solution)/shard_map/all_to_all | solution.py:334
  124.7 11.2 %collective-permute-start.10 = (bf16[256,128]{1,0:T(8,128)(2,1)S(1)}, bf16[256,128]{1,0:T(8,128)(2,1)S(1)}, u32[]{:S(2)}, u32[]{:S(2)}) collective-permute-start(bf16[256,128]{1,0:T(8,128)(2,1)S(1)} %shard_map.118.refs_0_), channel_id=1, source_target_pairs={{0,224},{32,0},{64,32},{96,64},{128,96},{160,128},{192,160},{224,1... | collective-permute-start | bytes 196616 | tf_op jit(solution)/shard_map/ppermute | solution.py:336
  126.7 10.8 %collective-permute-start.11 = (bf16[256,128]{1,0:T(8,128)(2,1)S(1)}, bf16[256,128]{1,0:T(8,128)(2,1)S(1)}, u32[]{:S(2)}, u32[]{:S(2)}) collective-permute-start(bf16[256,128]{1,0:T(8,128)(2,1)S(1)} %shard_map.118.refs_0_), channel_id=1, source_target_pairs={{0,64},{32,96},{64,128},{96,160},{128,192},{160,224},{192,0},{224,... | collective-permute-start | bytes 196616 | tf_op jit(solution)/shard_map/ppermute | solution.py:336
  126.7 14.2 %collective-permute-start.12 = (bf16[256,128]{1,0:T(8,128)(2,1)S(1)}, bf16[256,128]{1,0:T(8,128)(2,1)S(1)}, u32[]{:S(2)}, u32[]{:S(2)}) collective-permute-start(bf16[256,128]{1,0:T(8,128)(2,1)S(1)} %shard_map.118.refs_0_), channel_id=1, source_target_pairs={{0,192},{32,224},{64,0},{96,32},{128,64},{160,96},{192,128},{224,1... | collective-permute-start | bytes 196616 | tf_op jit(solution)/shard_map/ppermute | solution.py:336
  130.8 10.1 %collective-permute-start.13 = (bf16[256,128]{1,0:T(8,128)(2,1)S(1)}, bf16[256,128]{1,0:T(8,128)(2,1)S(1)}, u32[]{:S(2)}, u32[]{:S(2)}) collective-permute-start(bf16[256,128]{1,0:T(8,128)(2,1)S(1)} %shard_map.118.refs_0_), channel_id=1, source_target_pairs={{0,96},{32,128},{64,160},{96,192},{128,224},{160,0},{192,32},{224,... | collective-permute-start | bytes 196616 | tf_op jit(solution)/shard_map/ppermute | solution.py:336
  131.7 11.3 %collective-permute-start.14 = (bf16[256,128]{1,0:T(8,128)(2,1)S(1)}, bf16[256,128]{1,0:T(8,128)(2,1)S(1)}, u32[]{:S(2)}, u32[]{:S(2)}) collective-permute-start(bf16[256,128]{1,0:T(8,128)(2,1)S(1)} %shard_map.118.refs_0_), channel_id=1, source_target_pairs={{0,160},{32,192},{64,224},{96,0},{128,32},{160,64},{192,96},{224,1... | collective-permute-start | bytes 196616 | tf_op jit(solution)/shard_map/ppermute | solution.py:336
  135.9 8.2 %collective-permute-start.15 = (bf16[256,128]{1,0:T(8,128)(2,1)S(1)}, bf16[256,128]{1,0:T(8,128)(2,1)S(1)}, u32[]{:S(2)}, u32[]{:S(2)}) collective-permute-start(bf16[256,128]{1,0:T(8,128)(2,1)S(1)} %shard_map.118.refs_0_), channel_id=1, source_target_pairs={{0,128},{32,160},{64,192},{96,224},{128,0},{160,32},{192,64},{224,... | collective-permute-start | bytes 196616 | tf_op jit(solution)/shard_map/ppermute | solution.py:336
  137.5 6.6 %collective-permute-start.9 = (bf16[256,128]{1,0:T(8,128)(2,1)S(1)}, bf16[256,128]{1,0:T(8,128)(2,1)S(1)}, u32[]{:S(2)}, u32[]{:S(2)}) collective-permute-start(bf16[256,128]{1,0:T(8,128)(2,1)S(1)} %shard_map.118.refs_0_), channel_id=1, source_target_pairs={{0,32},{32,64},{64,96},{96,128},{128,160},{160,192},{192,224},{224... | collective-permute-start | bytes 196616 | tf_op jit(solution)/shard_map/ppermute | solution.py:336
  145.3 2.7 %collective-permute-start.18 = (bf16[256,2048]{1,0:T(8,128)(2,1)S(1)}, bf16[256,2048]{1,0:T(8,128)(2,1)S(1)}, u32[]{:S(2)}, u32[]{:S(2)}) collective-permute-start(bf16[256,2048]{1,0:T(8,128)(2,1)S(1)} %shard_map.121), channel_id=1, source_target_pairs={{0,1},{1,0},{2,3},{3,2},{4,5},{5,4},{6,7},{7,6},{8,9},{9,8},{10,11... | collective-permute-start | bytes 3145736 | tf_op jit(solution)/shard_map/ppermute | solution.py:226
  145.4 9.8 %copy-start.10 = (f32[256,1]{1,0:T(8,128)S(1)}, f32[256,1]{1,0:T(8,128)}, u32[]{:S(2)}) copy-start(f32[256,1]{1,0:T(8,128)} %convert_element_type.25.usable_ref) | copy-start | bytes 3076
  145.4 9.8 %copy-start.11 = (s32[256,1]{1,0:T(8,128)S(1)}, s32[256,1]{1,0:T(8,128)}, u32[]{:S(2)}) copy-start(s32[256,1]{1,0:T(8,128)} %add_subtract_fusion.next_ref) | copy-start | bytes 3076
  148.1 1.0 copy-start.6
  149.0 1.2 copy-start.7
  152.9 2.0 %collective-permute-start.19 = (f32[256,512]{1,0:T(8,128)S(1)}, f32[256,512]{1,0:T(8,128)S(1)}, u32[]{:S(2)}, u32[]{:S(2)}) collective-permute-start(f32[256,512]{1,0:T(8,128)S(1)} %get-tuple-element.60.near_ref), channel_id=1, source_target_pairs={{0,1},{1,0},{2,3},{3,2},{4,5},{5,4},{6,7},{7,6},{8,9},{9,8},{10,11... | collective-permute-start | bytes 1572872 | tf_op jit(solution)/shard_map/ppermute | solution.py:226
  153.2 0.8 copy-start.8
  154.9 11.0 %collective-permute-start.20 = (bf16[256,2048]{1,0:T(8,128)(2,1)S(1)}, bf16[256,2048]{1,0:T(8,128)(2,1)}, u32[]{:S(2)}, u32[]{:S(2)}) collective-permute-start(bf16[256,2048]{1,0:T(8,128)(2,1)S(1)} %get-tuple-element.68.user_ref), channel_id=1, source_target_pairs={{0,1},{1,0},{2,3},{3,2},{4,5},{5,4},{6,7},{7,6},{8,9},{9,8},{10,11... | collective-permute-start | bytes 3145736 | tf_op jit(solution)/shard_map/ppermute | solution.py:226
  155.2 1.0 copy-start.9
  158.3 25.5 %all-to-all-start.5 = ((bf16[16,16,2048]{2,1,0:T(8,128)(2,1)}), bf16[16,16,2048]{2,1,0:T(8,128)(2,1)S(1)}, u32[]{:S(2)}, u32[]{:S(2)}) async-start(bf16[16,16,2048]{2,1,0:T(8,128)(2,1)} %bitcast.8), calls=%async_computation.5 | async-start | bytes 2097152 | tf_op jit(solution)/shard_map/all_to_all | solution.py:387
